TPU v7x, 32 devices: a whole 2x2x4 slice. The times are simulated.
32 devices in a mesh: tok: 16 (over z, y, x), feat: 2 (over core).
Axes of the slice: x: 2, y: 2, z: 4, core: 2. Of those that a mesh axis runs over, the one named last changes fastest.
Arguments:
- activations: bfloat16 [32768, 8192], P('tok', 'feat')
- labels: int32 [32768], P('tok'), may hold values from 0 to 7, as said below
Outputs:
- cov_panel: float32 [256, 8192], P('tok', 'feat')
- cross_cov: float32 [8, 8192], P(None, 'feat')
Inputs may be any that keep to these rules, and one draw needn't show every extreme that they name: `labels`: each token's class.
All inputs are finite; a program needn't handle non-finite values.
Results may differ from a plain program's by a relative error of at most 0.0017.
Values may be sent and summed in bfloat16 or wider, within the bound.
No kernel may reach another device: no remote copies, remote signals or barrier semaphores. Data moves between devices by JAX's collectives and lax.ppermute only.
A program may use at most 64 MiB of HBM per device.

v0:
```python
import functools

import jax
import jax.numpy as jnp
from jax import lax
from jax.experimental import pallas as pl
from jax.experimental.pallas import tpu as pltpu
from jax.sharding import PartitionSpec as P

CLASSES = 8
PANEL = 128
PAD = 16
SHIFT_ROWS = 128
CHUNKS = (5, 3)
VMEM_LIMIT = 48 * 2**20
PIECES = 2
SUMS = -1


def orders_of(levels):
    even = list(range(levels))
    odd = list(even)
    for i in range(0, levels - 1, 2):
        odd[i], odd[i + 1] = even[i + 1], even[i]
    return even, odd


def position(block, order):
    pos = 0
    for bit in order:
        pos = pos * 2 + ((block >> bit) & 1)
    return pos


def prepare(orders, meta_ref, pieces, onehot_ref, left, columns, extra_ref):
    tokens = left.shape[1]
    rows = left.shape[0] - PAD
    unit = rows // 2 ** len(orders[0])
    for i, piece in enumerate(pieces):
        size = piece.shape[1]
        raw = piece[...].T
        shift = jnp.mean(raw[:, :SHIFT_ROWS].astype(jnp.float32), axis=1, keepdims=True)
        shift = shift.astype(jnp.bfloat16)
        y = raw - shift
        shift = jnp.broadcast_to(shift.astype(jnp.float32), (size, PANEL))
        first = meta_ref[i]
        for j in range(size // unit):
            block = first + j
            even, odd = (
                sum(((block >> bit) & 1) << k for k, bit in enumerate(reversed(order)))
                for order in orders
            )
            pos = jnp.where(meta_ref[len(pieces) + 1] == 0, even, odd)
            at = pl.ds(pl.multiple_of(pos * unit, unit), unit)
            here = slice(j * unit, (j + 1) * unit)
            left[at, :] = y[here]
            columns[at, :] = shift[here]
    left[rows:, :] = onehot_ref[...]
    shift = columns[:rows, :]
    total = jnp.sum(left[...].astype(jnp.float32), axis=1, keepdims=True)
    columns[...] = jnp.broadcast_to(total, columns.shape)
    extra_ref[...] = jnp.zeros(extra_ref.shape, jnp.float32)
    extra_ref[:, :PANEL] = columns[rows:rows + CLASSES, :]
    means = columns[:rows, :] / tokens + shift
    for i in range(rows // PANEL):
        extra_ref[i:i + 1, PANEL:] = means[i * PANEL:(i + 1) * PANEL].T[:1, :]


def local_kernel(first, blocks, orders, n_pieces, meta_ref, x_hbm, *refs):
    if first == 0:
        pieces, refs = refs[:n_pieces], refs[n_pieces:]
        onehot_ref, send_ref, keep_ref, sums_ref, means_ref, left, columns, extra_ref, split, x_vmem, sems = refs
    else:
        left, columns, send_ref, keep_ref, sums_ref, means_ref, split, x_vmem, sems = refs
    tokens, width = x_vmem.shape[1:]
    rows = left.shape[0] - PAD
    half = rows // 2
    size = tokens // PIECES
    copies = [
        [
            pltpu.make_async_copy(
                x_hbm.at[pl.ds(p * size, size), pl.ds((first + i) * width, width)],
                x_vmem.at[i, pl.ds(p * size, size), :],
                sems.at[i, p],
            )
            for p in range(PIECES)
        ]
        for i in range(blocks)
    ]
    for copy in copies:
        for piece in copy:
            piece.start()
    if first == 0:
        prepare(orders, meta_ref, pieces, onehot_ref, left, columns, extra_ref)

    mine = meta_ref[n_pieces]
    keep = pl.ds(pl.multiple_of(mine * half, half), half)
    send = pl.ds(pl.multiple_of((1 - mine) * half, half), half)
    for i, copy in enumerate(copies):
        for piece in copy:
            piece.wait()
        x = x_vmem[i]
        shift = jnp.mean(x[:SHIFT_ROWS].astype(jnp.float32), axis=0, keepdims=True).astype(jnp.bfloat16)
        out = jnp.dot(left[...], x - shift, preferred_element_type=jnp.float32)
        by_class = out[rows:rows + CLASSES]
        total = jnp.sum(by_class, axis=0, keepdims=True) / tokens
        shift = shift.astype(jnp.float32)
        here = slice(i * width, (i + 1) * width)
        sums_ref[:, here] = by_class + columns[rows:rows + CLASSES, :1] * shift
        means_ref[i:i + 1, :] = total + shift
        split[...] = out[:rows] - columns[:rows, :1] * total
        keep_ref[:, here] = split[keep, :]
        send_ref[:, here] = split[send, :].astype(jnp.bfloat16)


def local_part(first, blocks, activations, pieces, onehot, meta, orders, rows, prepared=None):
    tokens, cols = activations.shape
    width = cols // CLASSES
    part = blocks * width
    vmem = pl.BlockSpec(memory_space=pltpu.VMEM)
    out_shape = [
        jax.ShapeDtypeStruct((rows // 2, part), jnp.bfloat16),
        jax.ShapeDtypeStruct((rows // 2, part), jnp.float32),
        jax.ShapeDtypeStruct((CLASSES, part), jnp.float32),
        jax.ShapeDtypeStruct((blocks, width), jnp.float32),
    ]
    if prepared is None:
        out_shape += [
            jax.ShapeDtypeStruct((rows + PAD, tokens), jnp.bfloat16),
            jax.ShapeDtypeStruct((rows + PAD, PANEL), jnp.float32),
            jax.ShapeDtypeStruct((CLASSES, 2 * PANEL), jnp.float32),
        ]
        args = list(pieces) + [onehot]
    else:
        args = list(prepared)
    return pl.pallas_call(
        functools.partial(local_kernel, first, blocks, orders, len(pieces)),
        in_specs=[pl.BlockSpec(memory_space=pltpu.SMEM), pl.BlockSpec(memory_space=pl.ANY)]
        + [vmem] * len(args),
        out_specs=[vmem] * len(out_shape),
        scratch_shapes=[
            pltpu.VMEM((rows, width), jnp.float32),
            pltpu.VMEM((blocks, tokens, width), jnp.bfloat16),
            pltpu.SemaphoreType.DMA((blocks, PIECES)),
        ],
        out_shape=out_shape,
        compiler_params=pltpu.CompilerParams(vmem_limit_bytes=VMEM_LIMIT),
        cost_estimate=pl.CostEstimate(
            flops=2 * tokens * part * (rows + PAD),
            bytes_accessed=2 * tokens * part + 6 * (rows // 2) * part,
            transcendentals=0,
        ),
        name="local_sums",
    )(meta, activations, *args)


def after(value, *others):
    return lax.optimization_barrier((value, *others))[0]


def body(activations, labels):
    tokens, cols = activations.shape
    n_tok, n_feat = lax.axis_size("tok"), lax.axis_size("feat")
    levels = n_tok.bit_length() - 1
    assert n_tok == 1 << levels
    rows = PANEL * n_feat
    unit = rows // n_tok
    me, feat = lax.axis_index("tok"), lax.axis_index("feat")
    total = tokens * n_tok
    even, odd = orders_of(levels)
    parity = feat % 2
    bits = [(me >> jnp.where(parity == 0, a, b)) & 1 for a, b in zip(even, odd)]

    def swap(value, level):
        pairs = []
        for i in range(n_tok):
            for f in range(n_feat):
                bit = (even, odd)[f % 2][level]
                pairs.append((i * n_feat + f, (i ^ (1 << bit)) * n_feat + f))
        return lax.ppermute(value, ("tok", "feat"), pairs)

    own = activations[:, :PANEL]
    if n_feat == 2:
        other = lax.ppermute(own, "feat", [(0, 1), (1, 0)])
        pieces = [own, other]
        places = [feat * PANEL // unit, (1 - feat) * PANEL // unit]
    else:
        pieces = [lax.all_gather(own, "feat", axis=1, tiled=True)]
        places = [0]
    meta = jnp.stack(places + [bits[0], parity]).astype(jnp.int32)
    onehot = (labels[None, :] == jnp.arange(PAD, dtype=jnp.int32)[:, None]).astype(jnp.bfloat16)

    sends, kept, sums, means, prepared = [], [], [], [], None
    for chunk, blocks in enumerate(CHUNKS):
        first = sum(CHUNKS[:chunk])
        out = local_part(first, blocks, activations, pieces, onehot, meta, (even, odd), rows, prepared)
        sends.append(out[0])
        kept.append(out[1])
        sums.append(out[2])
        means.append(out[3])
        if chunk == 0:
            prepared, extra = out[4:6], out[6]
    head, lanes = cols + PANEL, cols // CLASSES
    sums = jnp.concatenate(
        sums + [extra[:, :PANEL], jnp.concatenate(means, axis=0), extra[:, PANEL:]], axis=1
    )

    start = sum(bit * (rows >> (k + 1)) for k, bit in enumerate(bits))
    last = len(CHUNKS) - 1
    turns = []
    for level in range(levels - 1):
        turns += [(chunk, level) for chunk in range(last)]
        turns.insert(len(turns) - (level == 1), (SUMS, level))
        turns += [(last, level)]
    turns += [(SUMS, levels - 1)]

    came = [swap(send, 0) for send in sends]
    route = list(range(2, levels)) + [1, 0]
    came_sums = swap(sums, route[0])
    done = ()
    for chunk, level in turns:
        if chunk == SUMS:
            other = after(came_sums, *done)
            sums = jnp.concatenate([sums[:, :head] + other[:, :head], sums[:, head:], other[:, head:]], axis=1)
            if level + 1 < levels:
                came_sums = swap(sums, route[level + 1])
            done = (sums,)
        else:
            mine, other = kept[chunk], after(came[chunk], *done)
            half = mine.shape[0] // 2
            bit = bits[level + 1]

            def merged(bit):
                pick = lambda a: lax.dynamic_slice_in_dim(a, bit * half, half, 0)
                return pick(mine) + pick(other).astype(jnp.float32)

            send = merged(1 - bit).astype(jnp.bfloat16)
            kept[chunk] = merged(bit)
            came[chunk] = swap(send, level + 1)
            done = (send,)

    means = sums[:, head:].reshape(CLASSES, n_tok, lanes + PANEL)
    away = (means - jnp.mean(means, axis=1, keepdims=True)).transpose(1, 0, 2)
    place = lax.dynamic_slice(
        away, (0, start // PANEL, lanes + start % PANEL), (n_tok, 1, unit)
    ).reshape(n_tok, unit)
    between = lax.dot_general(
        place, away[:, :, :lanes].reshape(n_tok, cols), (((0,), (0,)), ((), ())),
        precision=lax.Precision.HIGHEST, preferred_element_type=jnp.float32,
    ) * (tokens / (total - 1))
    by_class, count = sums[:, :cols], sums[:, cols:cols + 1]
    cross_cov = (by_class - count * (jnp.sum(by_class, axis=0) / total)) / total
    came = [after(c, between, cross_cov) for c in came]
    cov_panel = jnp.concatenate(
        [mine + other.astype(jnp.float32) for mine, other in zip(kept, came)], axis=1
    ) / (total - 1) + between
    return cov_panel, cross_cov


def solution(mesh):
    in_specs = (P("tok", "feat"), P("tok"))
    out_specs = (P("tok", "feat"), P(None, "feat"))
    return jax.shard_map(body, mesh=mesh, in_specs=in_specs, out_specs=out_specs, check_vma=False)
```

profile of v0, /device:TPU:0, one launch (start us, length us, event | category | flops | bytes accessed | tf_op | source)
XLA Modules:
  0.0 51.9 jit_solution(11695278266237335808)
XLA Ops:
  0.6 1.1 %slice.52.refs_0_ = bf16[2048,128]{1,0:T(8,128)(2,1)S(1)} slice(bf16[2048,4096]{1,0:T(8,128)(2,1)} %x_hbm.3), slice={[0:2048], [0:128]} | slice | bytes 1048576 | tf_op jit(solution)/shard_map/slice | solution.py:182
  1.7 0.5 collective-permute-start
  2.3 0.7 %fusion.1.refs_2_ = bf16[16,2048]{1,0:T(8,128)(2,1)S(1)} fusion(s32[2048]{0:T(1024)} %param.3), kind=kLoop, calls=%fused_computation.22 | loop fusion | flops 65536 | bytes 73728 | tf_op jit(solution)/shard_map/convert_element_type | solution.py:191
  3.0 0.7 %collective-permute-done.refs_1_ = bf16[2048,128]{1,0:T(8,128)(2,1)S(1)} collective-permute-done((bf16[2048,128]{1,0:T(8,128)(2,1)S(1)}, bf16[2048,128]{1,0:T(8,128)(2,1)S(1)}, u32[]{:S(2)}, u32[]{:S(2)}) %collective-permute-start) | collective-permute-done | bytes 524320 | tf_op jit(solution)/shard_map/ppermute | solution.py:184
  3.8 7.3 %local_sums.2 = (bf16[128,2560]{1,0:T(8,128)(2,1)S(1)}, f32[128,2560]{1,0:T(8,128)S(1)}, f32[8,2560]{1,0:T(8,128)S(1)}, f32[5,512]{1,0:T(8,128)S(1)}, bf16[272,2...) custom-call(s32[4]{0:T(128)S(1)} %pad_add_fusion.meta_ref, bf16[2048,4096]{1,0:T(8,128)(2,1)} %x_hbm.3, ...), custom_call_target="tpu_custom_call" | custom-call | flops 2852126720 | bytes 12451840 | tf_op jit(solution)/shard_map/local_sums/pallas_call | solution.py:136
  11.1 2.9 %collective-permute-start.1 = (bf16[128,2560]{1,0:T(8,128)(2,1)S(1)}, bf16[128,2560]{1,0:T(8,128)(2,1)S(1)}, u32[]{:S(2)}, u32[]{:S(2)}) collective-permute-start(bf16[128,2560]{1,0:T(8,128)(2,1)S(1)} %get-tuple-element.25), channel_id=1, source_target_pairs={{0,2},{1,5},{2,0},{3,7},{4,6},{5,1},{6,4},{7,3},{8,10},{9,13},{10,... | collective-permute-start | bytes 1966088 | tf_op jit(solution)/shard_map/ppermute | solution.py:180
  14.0 4.9 %local_sums.3 = (bf16[128,1536]{1,0:T(8,128)(2,1)S(1)}, f32[128,1536]{1,0:T(8,128)S(1)}, f32[8,1536]{1,0:T(8,128)S(1)}, f32[3,512]{1,0:T(4,128)S(1)}) custom-call(s32[4]{0:T(128)S(1)} %pad_add_fusion.meta_ref, bf16[2048,4096]{1,0:T(8,128)(2,1)} %x_hbm.3, bf16[272,2048]{1,0:T(8,128)(2,1)S(1)} %get-tuple-element.27.refs_0_, ...), custom_call_target="tpu_custom_call" | custom-call | flops 1711276032 | bytes 7471104 | tf_op jit(solution)/shard_map/local_sums/pallas_call | solution.py:136
  19.0 1.6 %collective-permute-start.3 = (f32[8,4864]{1,0:T(8,128)S(1)}, f32[8,4864]{1,0:T(8,128)S(1)}, u32[]{:S(2)}, u32[]{:S(2)}) collective-permute-start(f32[8,4864]{1,0:T(8,128)S(1)} %get-tuple-element.65), channel_id=1, source_target_pairs={{0,8},{1,17},{2,10},{3,19},{4,12},{5,21},{6,14},{7,23},{8,0},{9,25... | collective-permute-start | bytes 466952 | tf_op jit(solution)/shard_map/ppermute | solution.py:180
  20.6 0.5 %collective-permute-start.5 = (bf16[128,1536]{1,0:T(8,128)(2,1)S(1)}, bf16[128,1536]{1,0:T(8,128)(2,1)S(1)}, u32[]{:S(2)}, u32[]{:S(2)}) collective-permute-start(bf16[128,1536]{1,0:T(8,128)(2,1)S(1)} %get-tuple-element.35), channel_id=1, source_target_pairs={{0,2},{1,5},{2,0},{3,7},{4,6},{5,1},{6,4},{7,3},{8,10},{9,13},{10,... | collective-permute-start | bytes 1179656 | tf_op jit(solution)/shard_map/ppermute | solution.py:180
  21.2 1.4 %collective-permute-done.1 = bf16[128,2560]{1,0:T(8,128)(2,1)S(1)} collective-permute-done((bf16[128,2560]{1,0:T(8,128)(2,1)S(1)}, bf16[128,2560]{1,0:T(8,128)(2,1)S(1)}, u32[]{:S(2)}, u32[]{:S(2)}) %collective-permute-start.1) | collective-permute-done | bytes 655392 | tf_op jit(solution)/shard_map/ppermute | solution.py:180
  22.7 2.1 %collective-permute-start.2 = (bf16[64,2560]{1,0:T(8,128)(2,1)S(1)}, bf16[64,2560]{1,0:T(8,128)(2,1)S(1)}, u32[]{:S(2)}, u32[]{:S(2)}) collective-permute-start(bf16[64,2560]{1,0:T(8,128)(2,1)S(1)} %get-tuple-element.47), channel_id=1, source_target_pairs={{0,4},{1,3},{2,6},{3,1},{4,0},{5,7},{6,2},{7,5},{8,12},{9,11},{10,... | collective-permute-start | bytes 983048 | tf_op jit(solution)/shard_map/ppermute | solution.py:180
  24.8 0.8 %collective-permute-done.3 = f32[8,4864]{1,0:T(8,128)S(1)} collective-permute-done((f32[8,4864]{1,0:T(8,128)S(1)}, f32[8,4864]{1,0:T(8,128)S(1)}, u32[]{:S(2)}, u32[]{:S(2)}) %collective-permute-start.3) | collective-permute-done | bytes 155680 | tf_op jit(solution)/shard_map/ppermute | solution.py:180
  25.7 1.9 %collective-permute-start.4 = (f32[8,5504]{1,0:T(8,128)S(1)}, f32[8,5504]{1,0:T(8,128)S(1)}, u32[]{:S(2)}, u32[]{:S(2)}) collective-permute-start(f32[8,5504]{1,0:T(8,128)S(1)} %pad_maximum_fusion), channel_id=1, source_target_pairs={{0,16},{1,9},{2,18},{3,11},{4,20},{5,13},{6,22},{7,15},{8,24},{9,1... | collective-permute-start | bytes 528392 | tf_op jit(solution)/shard_map/ppermute | solution.py:180
  27.6 4.3 %collective-permute-done.5 = bf16[128,1536]{1,0:T(8,128)(2,1)S(1)} collective-permute-done((bf16[128,1536]{1,0:T(8,128)(2,1)S(1)}, bf16[128,1536]{1,0:T(8,128)(2,1)S(1)}, u32[]{:S(2)}, u32[]{:S(2)}) %collective-permute-start.5) | collective-permute-done | bytes 393248 | tf_op jit(solution)/shard_map/ppermute | solution.py:180
  31.9 1.3 %collective-permute-start.7 = (bf16[64,1536]{1,0:T(8,128)(2,1)S(1)}, bf16[64,1536]{1,0:T(8,128)(2,1)S(1)}, u32[]{:S(2)}, u32[]{:S(2)}) collective-permute-start(bf16[64,1536]{1,0:T(8,128)(2,1)S(1)} %get-tuple-element.49), channel_id=1, source_target_pairs={{0,4},{1,3},{2,6},{3,1},{4,0},{5,7},{6,2},{7,5},{8,12},{9,11},{10,... | collective-permute-start | bytes 589832 | tf_op jit(solution)/shard_map/ppermute | solution.py:180
  33.3 0.8 %collective-permute-start.9 = (f32[8,6784]{1,0:T(8,128)S(1)}, f32[8,6784]{1,0:T(8,128)S(1)}, u32[]{:S(2)}, u32[]{:S(2)}) collective-permute-start(f32[8,6784]{1,0:T(8,128)S(1)} %constant_dynamic-update-slice_fusion.5), channel_id=1, source_target_pairs={{0,4},{1,3},{2,6},{3,1},{4,0},{5,7},{6,2},{7,5},{8,12},{9,11},{10,... | collective-permute-start | bytes 651272 | tf_op jit(solution)/shard_map/ppermute | solution.py:180
  34.2 1.5 %collective-permute-start.6 = (bf16[32,2560]{1,0:T(8,128)(2,1)S(1)}, bf16[32,2560]{1,0:T(8,128)(2,1)S(1)}, u32[]{:S(2)}, u32[]{:S(2)}) collective-permute-start(bf16[32,2560]{1,0:T(8,128)(2,1)S(1)} %get-tuple-element.50), channel_id=1, source_target_pairs={{0,8},{1,17},{2,10},{3,19},{4,12},{5,21},{6,14},{7,23},{8,0},{9,25... | collective-permute-start | bytes 491528 | tf_op jit(solution)/shard_map/ppermute | solution.py:180
  35.7 1.9 %collective-permute-done.7 = bf16[64,1536]{1,0:T(8,128)(2,1)S(1)} collective-permute-done((bf16[64,1536]{1,0:T(8,128)(2,1)S(1)}, bf16[64,1536]{1,0:T(8,128)(2,1)S(1)}, u32[]{:S(2)}, u32[]{:S(2)}) %collective-permute-start.7) | collective-permute-done | bytes 196640 | tf_op jit(solution)/shard_map/ppermute | solution.py:180
  37.8 4.5 %collective-permute-done.6 = bf16[32,2560]{1,0:T(8,128)(2,1)S(1)} collective-permute-done((bf16[32,2560]{1,0:T(8,128)(2,1)S(1)}, bf16[32,2560]{1,0:T(8,128)(2,1)S(1)}, u32[]{:S(2)}, u32[]{:S(2)}) %collective-permute-start.6) | collective-permute-done | bytes 163872 | tf_op jit(solution)/shard_map/ppermute | solution.py:180
  42.9 1.5 %collective-permute-start.8 = (bf16[16,2560]{1,0:T(8,128)(2,1)S(1)}, bf16[16,2560]{1,0:T(8,128)(2,1)S(1)}, u32[]{:S(2)}, u32[]{:S(2)}) collective-permute-start(bf16[16,2560]{1,0:T(8,128)(2,1)S(1)} %add_convert_fusion.4), channel_id=1, source_target_pairs={{0,16},{1,9},{2,18},{3,11},{4,20},{5,13},{6,22},{7,15},{8,24},{9,1... | collective-permute-start | bytes 245768 | tf_op jit(solution)/shard_map/ppermute | solution.py:180
  44.4 1.5 %collective-permute-start.12 = (bf16[16,1536]{1,0:T(8,128)(2,1)S(1)}, bf16[16,1536]{1,0:T(8,128)(2,1)S(1)}, u32[]{:S(2)}, u32[]{:S(2)}) collective-permute-start(bf16[16,1536]{1,0:T(8,128)(2,1)S(1)} %add_convert_fusion.5), channel_id=1, source_target_pairs={{0,16},{1,9},{2,18},{3,11},{4,20},{5,13},{6,22},{7,15},{8,24},{9,1... | collective-permute-start | bytes 147464 | tf_op jit(solution)/shard_map/ppermute | solution.py:180
  45.9 3.4 %collective-permute-done.10 = f32[8,9344]{1,0:T(8,128)S(1)} collective-permute-done((f32[8,9344]{1,0:T(8,128)S(1)}, f32[8,9344]{1,0:T(8,128)S(1)}, u32[]{:S(2)}, u32[]{:S(2)}) %collective-permute-start.10) | collective-permute-done | bytes 299040 | tf_op jit(solution)/shard_map/ppermute | solution.py:180
  49.9 0.7 %subtract_multiply_fusion = f32[8,4096]{1,0:T(8,128)} fusion(f32[8,4224]{1,0:T(8,128)S(1)} %slice_add_fusion, f32[4096]{0:T(1024)S(1)} %broadcast_multiply_fusion.1, f32[8]{0:T(128)S(1)} %slice_reduce_fusion.1), kind=kLoop, calls=%fused_computation.20 | loop fusion | flops 98304 | bytes 278560 | tf_op jit(solution)/shard_map/div | solution.py:252
  51.2 0.7 %fusion = f32[16,4096]{1,0:T(8,128)} fusion(f32[16,4096]{1,0:T(8,128)S(1)} %convolution_multiply_fusion, f32[16,1536]{1,0:T(8,128)S(1)} %convert_add_fusion.5, f32[16,2560]{1,0:T(8,128)S(1)} %convert_add_fusion.4), kind=kLoop, calls=%fused_computation.8 | loop fusion | flops 196608 | bytes 786432 | tf_op jit(solution)/shard_map/add | solution.py:254
  (49 shorter events, 2.1 us)
Async XLA Ops:
  1.7 2.1 %collective-permute-start = (bf16[2048,128]{1,0:T(8,128)(2,1)S(1)}, bf16[2048,128]{1,0:T(8,128)(2,1)S(1)}, u32[]{:S(2)}, u32[]{:S(2)}) collective-permute-start(bf16[2048,128]{1,0:T(8,128)(2,1)S(1)} %slice.52.refs_0_), channel_id=1, source_target_pairs={{0,1},{1,0},{2,3},{3,2},{4,5},{5,4},{6,7},{7,6},{8,9},{9,8},{10,11... | collective-permute-start | bytes 1572872 | tf_op jit(solution)/shard_map/ppermute | solution.py:184
  11.1 11.5 %collective-permute-start.1 = (bf16[128,2560]{1,0:T(8,128)(2,1)S(1)}, bf16[128,2560]{1,0:T(8,128)(2,1)S(1)}, u32[]{:S(2)}, u32[]{:S(2)}) collective-permute-start(bf16[128,2560]{1,0:T(8,128)(2,1)S(1)} %get-tuple-element.25), channel_id=1, source_target_pairs={{0,2},{1,5},{2,0},{3,7},{4,6},{5,1},{6,4},{7,3},{8,10},{9,13},{10,... | collective-permute-start | bytes 1966088 | tf_op jit(solution)/shard_map/ppermute | solution.py:180
  19.0 6.6 %collective-permute-start.3 = (f32[8,4864]{1,0:T(8,128)S(1)}, f32[8,4864]{1,0:T(8,128)S(1)}, u32[]{:S(2)}, u32[]{:S(2)}) collective-permute-start(f32[8,4864]{1,0:T(8,128)S(1)} %get-tuple-element.65), channel_id=1, source_target_pairs={{0,8},{1,17},{2,10},{3,19},{4,12},{5,21},{6,14},{7,23},{8,0},{9,25... | collective-permute-start | bytes 466952 | tf_op jit(solution)/shard_map/ppermute | solution.py:180
  20.6 11.2 %collective-permute-start.5 = (bf16[128,1536]{1,0:T(8,128)(2,1)S(1)}, bf16[128,1536]{1,0:T(8,128)(2,1)S(1)}, u32[]{:S(2)}, u32[]{:S(2)}) collective-permute-start(bf16[128,1536]{1,0:T(8,128)(2,1)S(1)} %get-tuple-element.35), channel_id=1, source_target_pairs={{0,2},{1,5},{2,0},{3,7},{4,6},{5,1},{6,4},{7,3},{8,10},{9,13},{10,... | collective-permute-start | bytes 1179656 | tf_op jit(solution)/shard_map/ppermute | solution.py:180
  22.7 11.5 %collective-permute-start.2 = (bf16[64,2560]{1,0:T(8,128)(2,1)S(1)}, bf16[64,2560]{1,0:T(8,128)(2,1)S(1)}, u32[]{:S(2)}, u32[]{:S(2)}) collective-permute-start(bf16[64,2560]{1,0:T(8,128)(2,1)S(1)} %get-tuple-element.47), channel_id=1, source_target_pairs={{0,4},{1,3},{2,6},{3,1},{4,0},{5,7},{6,2},{7,5},{8,12},{9,11},{10,... | collective-permute-start | bytes 983048 | tf_op jit(solution)/shard_map/ppermute | solution.py:180
  25.7 7.6 %collective-permute-start.4 = (f32[8,5504]{1,0:T(8,128)S(1)}, f32[8,5504]{1,0:T(8,128)S(1)}, u32[]{:S(2)}, u32[]{:S(2)}) collective-permute-start(f32[8,5504]{1,0:T(8,128)S(1)} %pad_maximum_fusion), channel_id=1, source_target_pairs={{0,16},{1,9},{2,18},{3,11},{4,20},{5,13},{6,22},{7,15},{8,24},{9,1... | collective-permute-start | bytes 528392 | tf_op jit(solution)/shard_map/ppermute | solution.py:180
  31.9 5.7 %collective-permute-start.7 = (bf16[64,1536]{1,0:T(8,128)(2,1)S(1)}, bf16[64,1536]{1,0:T(8,128)(2,1)S(1)}, u32[]{:S(2)}, u32[]{:S(2)}) collective-permute-start(bf16[64,1536]{1,0:T(8,128)(2,1)S(1)} %get-tuple-element.49), channel_id=1, source_target_pairs={{0,4},{1,3},{2,6},{3,1},{4,0},{5,7},{6,2},{7,5},{8,12},{9,11},{10,... | collective-permute-start | bytes 589832 | tf_op jit(solution)/shard_map/ppermute | solution.py:180
  33.3 9.0 %collective-permute-start.9 = (f32[8,6784]{1,0:T(8,128)S(1)}, f32[8,6784]{1,0:T(8,128)S(1)}, u32[]{:S(2)}, u32[]{:S(2)}) collective-permute-start(f32[8,6784]{1,0:T(8,128)S(1)} %constant_dynamic-update-slice_fusion.5), channel_id=1, source_target_pairs={{0,4},{1,3},{2,6},{3,1},{4,0},{5,7},{6,2},{7,5},{8,12},{9,11},{10,... | collective-permute-start | bytes 651272 | tf_op jit(solution)/shard_map/ppermute | solution.py:180
  34.2 8.1 %collective-permute-start.6 = (bf16[32,2560]{1,0:T(8,128)(2,1)S(1)}, bf16[32,2560]{1,0:T(8,128)(2,1)S(1)}, u32[]{:S(2)}, u32[]{:S(2)}) collective-permute-start(bf16[32,2560]{1,0:T(8,128)(2,1)S(1)} %get-tuple-element.50), channel_id=1, source_target_pairs={{0,8},{1,17},{2,10},{3,19},{4,12},{5,21},{6,14},{7,23},{8,0},{9,25... | collective-permute-start | bytes 491528 | tf_op jit(solution)/shard_map/ppermute | solution.py:180
  37.7 6.7 %collective-permute-start.11 = (bf16[32,1536]{1,0:T(8,128)(2,1)S(1)}, bf16[32,1536]{1,0:T(8,128)(2,1)S(1)}, u32[]{:S(2)}, u32[]{:S(2)}) collective-permute-start(bf16[32,1536]{1,0:T(8,128)(2,1)S(1)} %get-tuple-element.53), channel_id=1, source_target_pairs={{0,8},{1,17},{2,10},{3,19},{4,12},{5,21},{6,14},{7,23},{8,0},{9,25... | collective-permute-start | bytes 294920 | tf_op jit(solution)/shard_map/ppermute | solution.py:180
  42.5 6.8 %collective-permute-start.10 = (f32[8,9344]{1,0:T(8,128)S(1)}, f32[8,9344]{1,0:T(8,128)S(1)}, u32[]{:S(2)}, u32[]{:S(2)}) collective-permute-start(f32[8,9344]{1,0:T(8,128)S(1)} %get-tuple-element.54), channel_id=1, source_target_pairs={{0,2},{1,5},{2,0},{3,7},{4,6},{5,1},{6,4},{7,3},{8,10},{9,13},{10,... | collective-permute-start | bytes 897032 | tf_op jit(solution)/shard_map/ppermute | solution.py:180
  42.9 8.2 %collective-permute-start.8 = (bf16[16,2560]{1,0:T(8,128)(2,1)S(1)}, bf16[16,2560]{1,0:T(8,128)(2,1)S(1)}, u32[]{:S(2)}, u32[]{:S(2)}) collective-permute-start(bf16[16,2560]{1,0:T(8,128)(2,1)S(1)} %add_convert_fusion.4), channel_id=1, source_target_pairs={{0,16},{1,9},{2,18},{3,11},{4,20},{5,13},{6,22},{7,15},{8,24},{9,1... | collective-permute-start | bytes 245768 | tf_op jit(solution)/shard_map/ppermute | solution.py:180
  44.4 6.7 %collective-permute-start.12 = (bf16[16,1536]{1,0:T(8,128)(2,1)S(1)}, bf16[16,1536]{1,0:T(8,128)(2,1)S(1)}, u32[]{:S(2)}, u32[]{:S(2)}) collective-permute-start(bf16[16,1536]{1,0:T(8,128)(2,1)S(1)} %add_convert_fusion.5), channel_id=1, source_target_pairs={{0,16},{1,9},{2,18},{3,11},{4,20},{5,13},{6,22},{7,15},{8,24},{9,1... | collective-permute-start | bytes 147464 | tf_op jit(solution)/shard_map/ppermute | solution.py:180
where the time goes:
time: 52.2 us; the launch traced here: 51.9 us
  waiting for transfers between devices  17.1 us (33%)
  starting transfers between devices  16.8 us (32%)
  Pallas kernels  12.2 us (23%)
  other arithmetic  2.97 us (6%)
  local copies, waits for them, and re-layouts  1.54 us (3%)
  between operations  0.91 us (2%)
    ppermute x12, waiting for transfers between devices, swap(): return lax.ppermute(value, ('tok', 'feat'), pairs)  16.4 us
    ppermute x12, starting transfers between devices, swap(): return lax.ppermute(value, ('tok', 'feat'), pairs)  16.3 us
    pallas_call x2, Pallas kernels, local_part(): pl.pallas_call(functools.partial(local_kernel, first, blocks, orders, len...  12.2 us
    slice x1, local copies, waits for them, and re-layouts, body(): own = activations[:, :PANEL]  1.08 us
  transfers between devices with their start and end apart: 13, of which 7 were waited for; matrix products, arithmetic and copies ran while one was open for 6% of the time, Pallas kernels for 9%

commit v1 on v0

--- a/solution.py
+++ b/solution.py
@@ -210,7 +210,7 @@
     turns = []
     for level in range(levels - 1):
         turns += [(chunk, level) for chunk in range(last)]
-        turns.insert(len(turns) - (level == 1), (SUMS, level))
+        turns.insert(len(turns) - (level == 2), (SUMS, level))
         turns += [(last, level)]
     turns += [(SUMS, levels - 1)]
 

time: 52.2 us -> 49.8 us (0.954)
  waiting for transfers between devices: 17.1 us -> 14.6 us
    ppermute x12, waiting for transfers between devices: 16.4 us -> 13.9 us  [swap(): return lax.ppermute(value, ('tok', 'feat'), pairs)]
  transfers between devices with their start and end apart: 13 -> 13, of which waited for: 7 -> 8; matrix products, arithmetic and copies ran while one was open for 6% -> 6% of each run, Pallas kernels for 9% -> 10%
where the time goes in v1:
time: 49.8 us; the launch traced here: 49.6 us
  starting transfers between devices  16.9 us (34%)
  waiting for transfers between devices  14.6 us (29%)
  Pallas kernels  12.2 us (24%)
  other arithmetic  2.96 us (6%)
  local copies, waits for them, and re-layouts  1.54 us (3%)
  between operations  0.92 us (2%)
    ppermute x12, starting transfers between devices, swap(): return lax.ppermute(value, ('tok', 'feat'), pairs)  16.4 us
    ppermute x12, waiting for transfers between devices, swap(): return lax.ppermute(value, ('tok', 'feat'), pairs)  13.9 us
    pallas_call x2, Pallas kernels, local_part(): pl.pallas_call(functools.partial(local_kernel, first, blocks, orders, len...  12.2 us
    slice x1, local copies, waits for them, and re-layouts, body(): own = activations[:, :PANEL]  1.08 us
  transfers between devices with their start and end apart: 13, of which 8 were waited for; matrix products, arithmetic and copies ran while one was open for 6% of the time, Pallas kernels for 10%

profile of v1, /device:TPU:0, one launch (start us, length us, event | category | flops | bytes accessed | tf_op | source)
XLA Modules:
  0.0 49.6 jit_solution(11071363633851610947)
XLA Ops:
  0.6 1.1 %slice.52.refs_0_ = bf16[2048,128]{1,0:T(8,128)(2,1)S(1)} slice(bf16[2048,4096]{1,0:T(8,128)(2,1)} %x_hbm.3), slice={[0:2048], [0:128]} | slice | bytes 1048576 | tf_op jit(solution)/shard_map/slice | solution.py:182
  1.7 0.5 %collective-permute-start = (bf16[2048,128]{1,0:T(8,128)(2,1)S(1)}, bf16[2048,128]{1,0:T(8,128)(2,1)S(1)}, u32[]{:S(2)}, u32[]{:S(2)}) collective-permute-start(bf16[2048,128]{1,0:T(8,128)(2,1)S(1)} %slice.52.refs_0_), channel_id=1, source_target_pairs={{0,1},{1,0},{2,3},{3,2},{4,5},{5,4},{6,7},{7,6},{8,9},{9,8},{10,11... | collective-permute-start | bytes 1572872 | tf_op jit(solution)/shard_map/ppermute | solution.py:184
  2.3 0.7 %fusion.1.refs_2_ = bf16[16,2048]{1,0:T(8,128)(2,1)S(1)} fusion(s32[2048]{0:T(1024)} %param.3), kind=kLoop, calls=%fused_computation.22 | loop fusion | flops 65536 | bytes 73728 | tf_op jit(solution)/shard_map/convert_element_type | solution.py:191
  3.0 0.7 %collective-permute-done.refs_1_ = bf16[2048,128]{1,0:T(8,128)(2,1)S(1)} collective-permute-done((bf16[2048,128]{1,0:T(8,128)(2,1)S(1)}, bf16[2048,128]{1,0:T(8,128)(2,1)S(1)}, u32[]{:S(2)}, u32[]{:S(2)}) %collective-permute-start) | collective-permute-done | bytes 524320 | tf_op jit(solution)/shard_map/ppermute | solution.py:184
  3.8 7.3 %local_sums.2 = (bf16[128,2560]{1,0:T(8,128)(2,1)S(1)}, f32[128,2560]{1,0:T(8,128)S(1)}, f32[8,2560]{1,0:T(8,128)S(1)}, f32[5,512]{1,0:T(8,128)S(1)}, bf16[272,2...) custom-call(s32[4]{0:T(128)S(1)} %pad_add_fusion.meta_ref, bf16[2048,4096]{1,0:T(8,128)(2,1)} %x_hbm.3, ...), custom_call_target="tpu_custom_call" | custom-call | flops 2852126720 | bytes 12451840 | tf_op jit(solution)/shard_map/local_sums/pallas_call | solution.py:136
  11.1 2.9 %collective-permute-start.1 = (bf16[128,2560]{1,0:T(8,128)(2,1)S(1)}, bf16[128,2560]{1,0:T(8,128)(2,1)S(1)}, u32[]{:S(2)}, u32[]{:S(2)}) collective-permute-start(bf16[128,2560]{1,0:T(8,128)(2,1)S(1)} %get-tuple-element.25), channel_id=1, source_target_pairs={{0,2},{1,5},{2,0},{3,7},{4,6},{5,1},{6,4},{7,3},{8,10},{9,13},{10,... | collective-permute-start | bytes 1966088 | tf_op jit(solution)/shard_map/ppermute | solution.py:180
  14.0 4.9 %local_sums.3 = (bf16[128,1536]{1,0:T(8,128)(2,1)S(1)}, f32[128,1536]{1,0:T(8,128)S(1)}, f32[8,1536]{1,0:T(8,128)S(1)}, f32[3,512]{1,0:T(4,128)S(1)}) custom-call(s32[4]{0:T(128)S(1)} %pad_add_fusion.meta_ref, bf16[2048,4096]{1,0:T(8,128)(2,1)} %x_hbm.3, bf16[272,2048]{1,0:T(8,128)(2,1)S(1)} %get-tuple-element.26.refs_0_, ...), custom_call_target="tpu_custom_call" | custom-call | flops 1711276032 | bytes 7471104 | tf_op jit(solution)/shard_map/local_sums/pallas_call | solution.py:136
  19.0 1.6 %collective-permute-start.4 = (f32[8,4864]{1,0:T(8,128)S(1)}, f32[8,4864]{1,0:T(8,128)S(1)}, u32[]{:S(2)}, u32[]{:S(2)}) collective-permute-start(f32[8,4864]{1,0:T(8,128)S(1)} %get-tuple-element.65), channel_id=1, source_target_pairs={{0,8},{1,17},{2,10},{3,19},{4,12},{5,21},{6,14},{7,23},{8,0},{9,25... | collective-permute-start | bytes 466952 | tf_op jit(solution)/shard_map/ppermute | solution.py:180
  20.6 0.5 %collective-permute-start.3 = (bf16[128,1536]{1,0:T(8,128)(2,1)S(1)}, bf16[128,1536]{1,0:T(8,128)(2,1)S(1)}, u32[]{:S(2)}, u32[]{:S(2)}) collective-permute-start(bf16[128,1536]{1,0:T(8,128)(2,1)S(1)} %get-tuple-element.29), channel_id=1, source_target_pairs={{0,2},{1,5},{2,0},{3,7},{4,6},{5,1},{6,4},{7,3},{8,10},{9,13},{10,... | collective-permute-start | bytes 1179656 | tf_op jit(solution)/shard_map/ppermute | solution.py:180
  21.2 1.4 %collective-permute-done.1 = bf16[128,2560]{1,0:T(8,128)(2,1)S(1)} collective-permute-done((bf16[128,2560]{1,0:T(8,128)(2,1)S(1)}, bf16[128,2560]{1,0:T(8,128)(2,1)S(1)}, u32[]{:S(2)}, u32[]{:S(2)}) %collective-permute-start.1) | collective-permute-done | bytes 655392 | tf_op jit(solution)/shard_map/ppermute | solution.py:180
  22.7 2.1 %collective-permute-start.2 = (bf16[64,2560]{1,0:T(8,128)(2,1)S(1)}, bf16[64,2560]{1,0:T(8,128)(2,1)S(1)}, u32[]{:S(2)}, u32[]{:S(2)}) collective-permute-start(bf16[64,2560]{1,0:T(8,128)(2,1)S(1)} %get-tuple-element.47), channel_id=1, source_target_pairs={{0,4},{1,3},{2,6},{3,1},{4,0},{5,7},{6,2},{7,5},{8,12},{9,11},{10,... | collective-permute-start | bytes 983048 | tf_op jit(solution)/shard_map/ppermute | solution.py:180
  24.8 0.8 %collective-permute-done.4 = f32[8,4864]{1,0:T(8,128)S(1)} collective-permute-done((f32[8,4864]{1,0:T(8,128)S(1)}, f32[8,4864]{1,0:T(8,128)S(1)}, u32[]{:S(2)}, u32[]{:S(2)}) %collective-permute-start.4) | collective-permute-done | bytes 155680 | tf_op jit(solution)/shard_map/ppermute | solution.py:180
  25.7 1.9 %collective-permute-start.6 = (f32[8,5504]{1,0:T(8,128)S(1)}, f32[8,5504]{1,0:T(8,128)S(1)}, u32[]{:S(2)}, u32[]{:S(2)}) collective-permute-start(f32[8,5504]{1,0:T(8,128)S(1)} %pad_maximum_fusion), channel_id=1, source_target_pairs={{0,16},{1,9},{2,18},{3,11},{4,20},{5,13},{6,22},{7,15},{8,24},{9,1... | collective-permute-start | bytes 528392 | tf_op jit(solution)/shard_map/ppermute | solution.py:180
  27.6 4.3 %collective-permute-done.3 = bf16[128,1536]{1,0:T(8,128)(2,1)S(1)} collective-permute-done((bf16[128,1536]{1,0:T(8,128)(2,1)S(1)}, bf16[128,1536]{1,0:T(8,128)(2,1)S(1)}, u32[]{:S(2)}, u32[]{:S(2)}) %collective-permute-start.3) | collective-permute-done | bytes 393248 | tf_op jit(solution)/shard_map/ppermute | solution.py:180
  31.9 1.3 %collective-permute-start.8 = (bf16[64,1536]{1,0:T(8,128)(2,1)S(1)}, bf16[64,1536]{1,0:T(8,128)(2,1)S(1)}, u32[]{:S(2)}, u32[]{:S(2)}) collective-permute-start(bf16[64,1536]{1,0:T(8,128)(2,1)S(1)} %get-tuple-element.49), channel_id=1, source_target_pairs={{0,4},{1,3},{2,6},{3,1},{4,0},{5,7},{6,2},{7,5},{8,12},{9,11},{10,... | collective-permute-start | bytes 589832 | tf_op jit(solution)/shard_map/ppermute | solution.py:180
  33.5 0.8 %collective-permute-start.7 = (f32[8,6784]{1,0:T(8,128)S(1)}, f32[8,6784]{1,0:T(8,128)S(1)}, u32[]{:S(2)}, u32[]{:S(2)}) collective-permute-start(f32[8,6784]{1,0:T(8,128)S(1)} %constant_dynamic-update-slice_fusion.5), channel_id=1, source_target_pairs={{0,4},{1,3},{2,6},{3,1},{4,0},{5,7},{6,2},{7,5},{8,12},{9,11},{10,... | collective-permute-start | bytes 651272 | tf_op jit(solution)/shard_map/ppermute | solution.py:180
  34.3 3.3 %collective-permute-done.8 = bf16[64,1536]{1,0:T(8,128)(2,1)S(1)} collective-permute-done((bf16[64,1536]{1,0:T(8,128)(2,1)S(1)}, bf16[64,1536]{1,0:T(8,128)(2,1)S(1)}, u32[]{:S(2)}, u32[]{:S(2)}) %collective-permute-start.8) | collective-permute-done | bytes 196640 | tf_op jit(solution)/shard_map/ppermute | solution.py:180
  37.8 2.2 %collective-permute-done.7 = f32[8,6784]{1,0:T(8,128)S(1)} collective-permute-done((f32[8,6784]{1,0:T(8,128)S(1)}, f32[8,6784]{1,0:T(8,128)S(1)}, u32[]{:S(2)}, u32[]{:S(2)}) %collective-permute-start.7) | collective-permute-done | bytes 217120 | tf_op jit(solution)/shard_map/ppermute | solution.py:180
  40.1 0.8 %collective-permute-start.10 = (f32[8,9344]{1,0:T(8,128)S(1)}, f32[8,9344]{1,0:T(8,128)S(1)}, u32[]{:S(2)}, u32[]{:S(2)}) collective-permute-start(f32[8,9344]{1,0:T(8,128)S(1)} %get-tuple-element.54), channel_id=1, source_target_pairs={{0,2},{1,5},{2,0},{3,7},{4,6},{5,1},{6,4},{7,3},{8,10},{9,13},{10,... | collective-permute-start | bytes 897032 | tf_op jit(solution)/shard_map/ppermute | solution.py:180
  41.5 1.7 %collective-permute-start.9 = (bf16[16,2560]{1,0:T(8,128)(2,1)S(1)}, bf16[16,2560]{1,0:T(8,128)(2,1)S(1)}, u32[]{:S(2)}, u32[]{:S(2)}) collective-permute-start(bf16[16,2560]{1,0:T(8,128)(2,1)S(1)} %add_convert_fusion.4), channel_id=1, source_target_pairs={{0,16},{1,9},{2,18},{3,11},{4,20},{5,13},{6,22},{7,15},{8,24},{9,1... | collective-permute-start | bytes 245768 | tf_op jit(solution)/shard_map/ppermute | solution.py:180
  43.2 2.4 %collective-permute-start.12 = (bf16[16,1536]{1,0:T(8,128)(2,1)S(1)}, bf16[16,1536]{1,0:T(8,128)(2,1)S(1)}, u32[]{:S(2)}, u32[]{:S(2)}) collective-permute-start(bf16[16,1536]{1,0:T(8,128)(2,1)S(1)} %add_convert_fusion.5), channel_id=1, source_target_pairs={{0,16},{1,9},{2,18},{3,11},{4,20},{5,13},{6,22},{7,15},{8,24},{9,1... | collective-permute-start | bytes 147464 | tf_op jit(solution)/shard_map/ppermute | solution.py:180
  45.6 1.4 %collective-permute-done.10 = f32[8,9344]{1,0:T(8,128)S(1)} collective-permute-done((f32[8,9344]{1,0:T(8,128)S(1)}, f32[8,9344]{1,0:T(8,128)S(1)}, u32[]{:S(2)}, u32[]{:S(2)}) %collective-permute-start.10) | collective-permute-done | bytes 299040 | tf_op jit(solution)/shard_map/ppermute | solution.py:180
  47.5 0.7 %subtract_multiply_fusion = f32[8,4096]{1,0:T(8,128)} fusion(f32[8,4224]{1,0:T(8,128)S(1)} %slice_add_fusion, f32[4096]{0:T(1024)S(1)} %broadcast_multiply_fusion.1, f32[8]{0:T(128)S(1)} %slice_reduce_fusion.1), kind=kLoop, calls=%fused_computation.20 | loop fusion | flops 98304 | bytes 278560 | tf_op jit(solution)/shard_map/div | solution.py:252
  48.8 0.7 %fusion = f32[16,4096]{1,0:T(8,128)} fusion(f32[16,4096]{1,0:T(8,128)S(1)} %convolution_multiply_fusion, f32[16,1536]{1,0:T(8,128)S(1)} %convert_add_fusion.5, f32[16,2560]{1,0:T(8,128)S(1)} %convert_add_fusion.4), kind=kLoop, calls=%fused_computation.8 | loop fusion | flops 196608 | bytes 786432 | tf_op jit(solution)/shard_map/add | solution.py:254
  (49 shorter events, 2.3 us)
Async XLA Ops:
  1.7 2.1 %collective-permute-start = (bf16[2048,128]{1,0:T(8,128)(2,1)S(1)}, bf16[2048,128]{1,0:T(8,128)(2,1)S(1)}, u32[]{:S(2)}, u32[]{:S(2)}) collective-permute-start(bf16[2048,128]{1,0:T(8,128)(2,1)S(1)} %slice.52.refs_0_), channel_id=1, source_target_pairs={{0,1},{1,0},{2,3},{3,2},{4,5},{5,4},{6,7},{7,6},{8,9},{9,8},{10,11... | collective-permute-start | bytes 1572872 | tf_op jit(solution)/shard_map/ppermute | solution.py:184
  11.1 11.5 %collective-permute-start.1 = (bf16[128,2560]{1,0:T(8,128)(2,1)S(1)}, bf16[128,2560]{1,0:T(8,128)(2,1)S(1)}, u32[]{:S(2)}, u32[]{:S(2)}) collective-permute-start(bf16[128,2560]{1,0:T(8,128)(2,1)S(1)} %get-tuple-element.25), channel_id=1, source_target_pairs={{0,2},{1,5},{2,0},{3,7},{4,6},{5,1},{6,4},{7,3},{8,10},{9,13},{10,... | collective-permute-start | bytes 1966088 | tf_op jit(solution)/shard_map/ppermute | solution.py:180
  19.0 6.6 %collective-permute-start.4 = (f32[8,4864]{1,0:T(8,128)S(1)}, f32[8,4864]{1,0:T(8,128)S(1)}, u32[]{:S(2)}, u32[]{:S(2)}) collective-permute-start(f32[8,4864]{1,0:T(8,128)S(1)} %get-tuple-element.65), channel_id=1, source_target_pairs={{0,8},{1,17},{2,10},{3,19},{4,12},{5,21},{6,14},{7,23},{8,0},{9,25... | collective-permute-start | bytes 466952 | tf_op jit(solution)/shard_map/ppermute | solution.py:180
  20.6 11.2 %collective-permute-start.3 = (bf16[128,1536]{1,0:T(8,128)(2,1)S(1)}, bf16[128,1536]{1,0:T(8,128)(2,1)S(1)}, u32[]{:S(2)}, u32[]{:S(2)}) collective-permute-start(bf16[128,1536]{1,0:T(8,128)(2,1)S(1)} %get-tuple-element.29), channel_id=1, source_target_pairs={{0,2},{1,5},{2,0},{3,7},{4,6},{5,1},{6,4},{7,3},{8,10},{9,13},{10,... | collective-permute-start | bytes 1179656 | tf_op jit(solution)/shard_map/ppermute | solution.py:180
  22.7 10.5 %collective-permute-start.2 = (bf16[64,2560]{1,0:T(8,128)(2,1)S(1)}, bf16[64,2560]{1,0:T(8,128)(2,1)S(1)}, u32[]{:S(2)}, u32[]{:S(2)}) collective-permute-start(bf16[64,2560]{1,0:T(8,128)(2,1)S(1)} %get-tuple-element.47), channel_id=1, source_target_pairs={{0,4},{1,3},{2,6},{3,1},{4,0},{5,7},{6,2},{7,5},{8,12},{9,11},{10,... | collective-permute-start | bytes 983048 | tf_op jit(solution)/shard_map/ppermute | solution.py:180
  25.7 7.8 %collective-permute-start.6 = (f32[8,5504]{1,0:T(8,128)S(1)}, f32[8,5504]{1,0:T(8,128)S(1)}, u32[]{:S(2)}, u32[]{:S(2)}) collective-permute-start(f32[8,5504]{1,0:T(8,128)S(1)} %pad_maximum_fusion), channel_id=1, source_target_pairs={{0,16},{1,9},{2,18},{3,11},{4,20},{5,13},{6,22},{7,15},{8,24},{9,1... | collective-permute-start | bytes 528392 | tf_op jit(solution)/shard_map/ppermute | solution.py:180
  31.9 5.7 %collective-permute-start.8 = (bf16[64,1536]{1,0:T(8,128)(2,1)S(1)}, bf16[64,1536]{1,0:T(8,128)(2,1)S(1)}, u32[]{:S(2)}, u32[]{:S(2)}) collective-permute-start(bf16[64,1536]{1,0:T(8,128)(2,1)S(1)} %get-tuple-element.49), channel_id=1, source_target_pairs={{0,4},{1,3},{2,6},{3,1},{4,0},{5,7},{6,2},{7,5},{8,12},{9,11},{10,... | collective-permute-start | bytes 589832 | tf_op jit(solution)/shard_map/ppermute | solution.py:180
  33.3 8.1 %collective-permute-start.5 = (bf16[32,2560]{1,0:T(8,128)(2,1)S(1)}, bf16[32,2560]{1,0:T(8,128)(2,1)S(1)}, u32[]{:S(2)}, u32[]{:S(2)}) collective-permute-start(bf16[32,2560]{1,0:T(8,128)(2,1)S(1)} %get-tuple-element.51), channel_id=1, source_target_pairs={{0,8},{1,17},{2,10},{3,19},{4,12},{5,21},{6,14},{7,23},{8,0},{9,25... | collective-permute-start | bytes 491528 | tf_op jit(solution)/shard_map/ppermute | solution.py:180
  33.5 6.5 %collective-permute-start.7 = (f32[8,6784]{1,0:T(8,128)S(1)}, f32[8,6784]{1,0:T(8,128)S(1)}, u32[]{:S(2)}, u32[]{:S(2)}) collective-permute-start(f32[8,6784]{1,0:T(8,128)S(1)} %constant_dynamic-update-slice_fusion.5), channel_id=1, source_target_pairs={{0,4},{1,3},{2,6},{3,1},{4,0},{5,7},{6,2},{7,5},{8,12},{9,11},{10,... | collective-permute-start | bytes 651272 | tf_op jit(solution)/shard_map/ppermute | solution.py:180
  37.7 5.5 %collective-permute-start.11 = (bf16[32,1536]{1,0:T(8,128)(2,1)S(1)}, bf16[32,1536]{1,0:T(8,128)(2,1)S(1)}, u32[]{:S(2)}, u32[]{:S(2)}) collective-permute-start(bf16[32,1536]{1,0:T(8,128)(2,1)S(1)} %get-tuple-element.53), channel_id=1, source_target_pairs={{0,8},{1,17},{2,10},{3,19},{4,12},{5,21},{6,14},{7,23},{8,0},{9,25... | collective-permute-start | bytes 294920 | tf_op jit(solution)/shard_map/ppermute | solution.py:180
  40.1 6.8 %collective-permute-start.10 = (f32[8,9344]{1,0:T(8,128)S(1)}, f32[8,9344]{1,0:T(8,128)S(1)}, u32[]{:S(2)}, u32[]{:S(2)}) collective-permute-start(f32[8,9344]{1,0:T(8,128)S(1)} %get-tuple-element.54), channel_id=1, source_target_pairs={{0,2},{1,5},{2,0},{3,7},{4,6},{5,1},{6,4},{7,3},{8,10},{9,13},{10,... | collective-permute-start | bytes 897032 | tf_op jit(solution)/shard_map/ppermute | solution.py:180
  41.5 7.3 %collective-permute-start.9 = (bf16[16,2560]{1,0:T(8,128)(2,1)S(1)}, bf16[16,2560]{1,0:T(8,128)(2,1)S(1)}, u32[]{:S(2)}, u32[]{:S(2)}) collective-permute-start(bf16[16,2560]{1,0:T(8,128)(2,1)S(1)} %add_convert_fusion.4), channel_id=1, source_target_pairs={{0,16},{1,9},{2,18},{3,11},{4,20},{5,13},{6,22},{7,15},{8,24},{9,1... | collective-permute-start | bytes 245768 | tf_op jit(solution)/shard_map/ppermute | solution.py:180
  43.2 5.6 %collective-permute-start.12 = (bf16[16,1536]{1,0:T(8,128)(2,1)S(1)}, bf16[16,1536]{1,0:T(8,128)(2,1)S(1)}, u32[]{:S(2)}, u32[]{:S(2)}) collective-permute-start(bf16[16,1536]{1,0:T(8,128)(2,1)S(1)} %add_convert_fusion.5), channel_id=1, source_target_pairs={{0,16},{1,9},{2,18},{3,11},{4,20},{5,13},{6,22},{7,15},{8,24},{9,1... | collective-permute-start | bytes 147464 | tf_op jit(solution)/shard_map/ppermute | solution.py:180

commit v2 on v1

--- a/solution.py
+++ b/solution.py
@@ -154,6 +154,45 @@
     )(meta, activations, *args)
 
 
+def finish_kernel(total, tokens, n, sums_ref, place_ref, away_ref, *refs):
+    kept, came, (cov_hbm, cross_hbm, cov, cross, sems) = refs[:n], refs[n:2 * n], refs[2 * n:]
+    cols = cov.shape[1]
+    by_class = sums_ref[:, :cols]
+    mean = jnp.sum(by_class, axis=0, keepdims=True) / total
+    cross[...] = (by_class - sums_ref[:, cols:cols + 1] * mean) / total
+    cross_copy = pltpu.make_async_copy(cross, cross_hbm, sems.at[0])
+    cross_copy.start()
+    between = jnp.dot(
+        place_ref[...], away_ref[...],
+        precision=lax.Precision.HIGHEST, preferred_element_type=jnp.float32,
+    ) * (tokens / (total - 1))
+    first = 0
+    for mine, other in zip(kept, came):
+        here = slice(first, first + mine.shape[1])
+        within = mine[...] + other[...].astype(jnp.float32)
+        cov[:, here] = within / (total - 1) + between[:, here]
+        first += mine.shape[1]
+    cov_copy = pltpu.make_async_copy(cov, cov_hbm, sems.at[1])
+    cov_copy.start()
+    cross_copy.wait()
+    cov_copy.wait()
+
+
+def finish(total, tokens, sums, place, away, kept, came):
+    cols = away.shape[1]
+    shapes = [(place.shape[0], cols), (CLASSES, cols)]
+    args = [sums, place, away, *kept, *came]
+    return pl.pallas_call(
+        functools.partial(finish_kernel, total, tokens, len(kept)),
+        in_specs=[pl.BlockSpec(memory_space=pltpu.VMEM)] * len(args),
+        out_specs=[pl.BlockSpec(memory_space=pl.ANY)] * 2,
+        out_shape=[jax.ShapeDtypeStruct(s, jnp.float32) for s in shapes],
+        scratch_shapes=[pltpu.VMEM(s, jnp.float32) for s in shapes] + [pltpu.SemaphoreType.DMA((2,))],
+        compiler_params=pltpu.CompilerParams(vmem_limit_bytes=16 * 2**20),
+        name="finish",
+    )(*args)
+
+
 def after(value, *others):
     return lax.optimization_barrier((value, *others))[0]
 
@@ -243,18 +282,11 @@
     away = (means - jnp.mean(means, axis=1, keepdims=True)).transpose(1, 0, 2)
     place = lax.dynamic_slice(
         away, (0, start // PANEL, lanes + start % PANEL), (n_tok, 1, unit)
-    ).reshape(n_tok, unit)
-    between = lax.dot_general(
-        place, away[:, :, :lanes].reshape(n_tok, cols), (((0,), (0,)), ((), ())),
-        precision=lax.Precision.HIGHEST, preferred_element_type=jnp.float32,
-    ) * (tokens / (total - 1))
-    by_class, count = sums[:, :cols], sums[:, cols:cols + 1]
-    cross_cov = (by_class - count * (jnp.sum(by_class, axis=0) / total)) / total
-    came = [after(c, between, cross_cov) for c in came]
-    cov_panel = jnp.concatenate(
-        [mine + other.astype(jnp.float32) for mine, other in zip(kept, came)], axis=1
-    ) / (total - 1) + between
-    return cov_panel, cross_cov
+    ).reshape(n_tok, unit).T
+    away = away[:, :, :lanes].reshape(n_tok, cols)
+    sums = sums[:, :head]
+    came = [after(c, place, away, sums) for c in came]
+    return tuple(finish(total, tokens, sums, place, away, kept, came))
 
 
 def solution(mesh):

time: 49.8 us -> 49.6 us (level)
  other arithmetic: 2.96 us -> 1.4 us
  Pallas kernels: 12.2 us -> 13.4 us
  waiting for transfers between devices: 14.6 us -> 15.4 us
    pallas_call x0 -> x1, Pallas kernels: none -> 1.16 us  [finish(): pl.pallas_call(functools.partial(finish_kernel, total, tokens, len(kept))...]
    add x3 -> x0, other arithmetic: 0.79 us -> none  [the longest x1 0.73 us: body(): jnp.concatenate([mine + other.astype(jnp.float32) for mine, other in zip(...]
    ppermute x12, waiting for transfers between devices: 13.9 us -> 14.7 us  [swap(): return lax.ppermute(value, ('tok', 'feat'), pairs)]
    div x2 -> x0, other arithmetic: 0.75 us -> none  [body(): cross_cov = (by_class - count * (jnp.sum(by_class, axis=0) / total)) / total]
  transfers between devices with their start and end apart: 13 -> 13, of which waited for: 8 -> 9; matrix products, arithmetic and copies ran while one was open for 6% -> 4% of each run, Pallas kernels for 10% -> 10%
where the time goes in v2:
time: 49.6 us; the launch traced here: 49.4 us
  starting transfers between devices  16.9 us (34%)
  waiting for transfers between devices  15.4 us (31%)
  Pallas kernels  13.4 us (27%)
  local copies, waits for them, and re-layouts  1.5 us (3%)
  other arithmetic  1.4 us (3%)
  between operations  0.87 us (2%)
    ppermute x12, starting transfers between devices, swap(): return lax.ppermute(value, ('tok', 'feat'), pairs)  16.4 us
    ppermute x12, waiting for transfers between devices, swap(): return lax.ppermute(value, ('tok', 'feat'), pairs)  14.7 us
    pallas_call x2, Pallas kernels, local_part(): pl.pallas_call(functools.partial(local_kernel, first, blocks, orders, len...  12.2 us
    pallas_call x1, Pallas kernels, finish(): pl.pallas_call(functools.partial(finish_kernel, total, tokens, len(kept))...  1.16 us
    slice x1, local copies, waits for them, and re-layouts, body(): own = activations[:, :PANEL]  1.08 us
  transfers between devices with their start and end apart: 13, of which 9 were waited for; matrix products, arithmetic and copies ran while one was open for 4% of the time, Pallas kernels for 10%

profile of v2, /device:TPU:0, one launch (start us, length us, event | category | flops | bytes accessed | tf_op | source)
XLA Modules:
  0.0 49.4 jit_solution(1801494676215606691)
XLA Ops:
  0.6 1.1 %slice.46.refs_0_ = bf16[2048,128]{1,0:T(8,128)(2,1)S(1)} slice(bf16[2048,4096]{1,0:T(8,128)(2,1)} %x_hbm.3), slice={[0:2048], [0:128]} | slice | bytes 1048576 | tf_op jit(solution)/shard_map/slice | solution.py:221
  1.7 0.5 %collective-permute-start = (bf16[2048,128]{1,0:T(8,128)(2,1)S(1)}, bf16[2048,128]{1,0:T(8,128)(2,1)S(1)}, u32[]{:S(2)}, u32[]{:S(2)}) collective-permute-start(bf16[2048,128]{1,0:T(8,128)(2,1)S(1)} %slice.46.refs_0_), channel_id=1, source_target_pairs={{0,1},{1,0},{2,3},{3,2},{4,5},{5,4},{6,7},{7,6},{8,9},{9,8},{10,11... | collective-permute-start | bytes 1572872 | tf_op jit(solution)/shard_map/ppermute | solution.py:223
  2.3 0.7 %fusion.refs_2_ = bf16[16,2048]{1,0:T(8,128)(2,1)S(1)} fusion(s32[2048]{0:T(1024)} %param.3), kind=kLoop, calls=%fused_computation.18 | loop fusion | flops 65536 | bytes 73728 | tf_op jit(solution)/shard_map/convert_element_type | solution.py:230
  3.0 0.7 %collective-permute-done.refs_1_ = bf16[2048,128]{1,0:T(8,128)(2,1)S(1)} collective-permute-done((bf16[2048,128]{1,0:T(8,128)(2,1)S(1)}, bf16[2048,128]{1,0:T(8,128)(2,1)S(1)}, u32[]{:S(2)}, u32[]{:S(2)}) %collective-permute-start) | collective-permute-done | bytes 524320 | tf_op jit(solution)/shard_map/ppermute | solution.py:223
  3.8 7.3 %local_sums.2 = (bf16[128,2560]{1,0:T(8,128)(2,1)S(1)}, f32[128,2560]{1,0:T(8,128)S(1)}, f32[8,2560]{1,0:T(8,128)S(1)}, f32[5,512]{1,0:T(8,128)S(1)}, bf16[272,2...) custom-call(s32[4]{0:T(128)S(1)} %pad_add_fusion.meta_ref, bf16[2048,4096]{1,0:T(8,128)(2,1)} %x_hbm.3, ...), custom_call_target="tpu_custom_call" | custom-call | flops 2852126720 | bytes 12451840 | tf_op jit(solution)/shard_map/local_sums/pallas_call | solution.py:136
  11.1 2.9 %collective-permute-start.2 = (bf16[128,2560]{1,0:T(8,128)(2,1)S(1)}, bf16[128,2560]{1,0:T(8,128)(2,1)S(1)}, u32[]{:S(2)}, u32[]{:S(2)}) collective-permute-start(bf16[128,2560]{1,0:T(8,128)(2,1)S(1)} %get-tuple-element.32), channel_id=1, source_target_pairs={{0,2},{1,5},{2,0},{3,7},{4,6},{5,1},{6,4},{7,3},{8,10},{9,13},{10,... | collective-permute-start | bytes 1966088 | tf_op jit(solution)/shard_map/ppermute | solution.py:219
  14.0 4.9 %local_sums.3 = (bf16[128,1536]{1,0:T(8,128)(2,1)S(1)}, f32[128,1536]{1,0:T(8,128)S(1)}, f32[8,1536]{1,0:T(8,128)S(1)}, f32[3,512]{1,0:T(4,128)S(1)}) custom-call(s32[4]{0:T(128)S(1)} %pad_add_fusion.meta_ref, bf16[2048,4096]{1,0:T(8,128)(2,1)} %x_hbm.3, bf16[272,2048]{1,0:T(8,128)(2,1)S(1)} %get-tuple-element.25.refs_0_, ...), custom_call_target="tpu_custom_call" | custom-call | flops 1711276032 | bytes 7471104 | tf_op jit(solution)/shard_map/local_sums/pallas_call | solution.py:136
  19.0 1.6 %collective-permute-start.1 = (f32[8,4864]{1,0:T(8,128)S(1)}, f32[8,4864]{1,0:T(8,128)S(1)}, u32[]{:S(2)}, u32[]{:S(2)}) collective-permute-start(f32[8,4864]{1,0:T(8,128)S(1)} %get-tuple-element.69), channel_id=1, source_target_pairs={{0,8},{1,17},{2,10},{3,19},{4,12},{5,21},{6,14},{7,23},{8,0},{9,25... | collective-permute-start | bytes 466952 | tf_op jit(solution)/shard_map/ppermute | solution.py:219
  20.6 0.5 %collective-permute-start.5 = (bf16[128,1536]{1,0:T(8,128)(2,1)S(1)}, bf16[128,1536]{1,0:T(8,128)(2,1)S(1)}, u32[]{:S(2)}, u32[]{:S(2)}) collective-permute-start(bf16[128,1536]{1,0:T(8,128)(2,1)S(1)} %get-tuple-element.35), channel_id=1, source_target_pairs={{0,2},{1,5},{2,0},{3,7},{4,6},{5,1},{6,4},{7,3},{8,10},{9,13},{10,... | collective-permute-start | bytes 1179656 | tf_op jit(solution)/shard_map/ppermute | solution.py:219
  21.2 1.4 %collective-permute-done.2 = bf16[128,2560]{1,0:T(8,128)(2,1)S(1)} collective-permute-done((bf16[128,2560]{1,0:T(8,128)(2,1)S(1)}, bf16[128,2560]{1,0:T(8,128)(2,1)S(1)}, u32[]{:S(2)}, u32[]{:S(2)}) %collective-permute-start.2) | collective-permute-done | bytes 655392 | tf_op jit(solution)/shard_map/ppermute | solution.py:219
  22.7 2.1 %collective-permute-start.4 = (bf16[64,2560]{1,0:T(8,128)(2,1)S(1)}, bf16[64,2560]{1,0:T(8,128)(2,1)S(1)}, u32[]{:S(2)}, u32[]{:S(2)}) collective-permute-start(bf16[64,2560]{1,0:T(8,128)(2,1)S(1)} %get-tuple-element.47), channel_id=1, source_target_pairs={{0,4},{1,3},{2,6},{3,1},{4,0},{5,7},{6,2},{7,5},{8,12},{9,11},{10,... | collective-permute-start | bytes 983048 | tf_op jit(solution)/shard_map/ppermute | solution.py:219
  24.8 0.8 %collective-permute-done.1 = f32[8,4864]{1,0:T(8,128)S(1)} collective-permute-done((f32[8,4864]{1,0:T(8,128)S(1)}, f32[8,4864]{1,0:T(8,128)S(1)}, u32[]{:S(2)}, u32[]{:S(2)}) %collective-permute-start.1) | collective-permute-done | bytes 155680 | tf_op jit(solution)/shard_map/ppermute | solution.py:219
  25.7 1.9 %collective-permute-start.3 = (f32[8,5504]{1,0:T(8,128)S(1)}, f32[8,5504]{1,0:T(8,128)S(1)}, u32[]{:S(2)}, u32[]{:S(2)}) collective-permute-start(f32[8,5504]{1,0:T(8,128)S(1)} %pad_maximum_fusion), channel_id=1, source_target_pairs={{0,16},{1,9},{2,18},{3,11},{4,20},{5,13},{6,22},{7,15},{8,24},{9,1... | collective-permute-start | bytes 528392 | tf_op jit(solution)/shard_map/ppermute | solution.py:219
  27.6 4.3 %collective-permute-done.5 = bf16[128,1536]{1,0:T(8,128)(2,1)S(1)} collective-permute-done((bf16[128,1536]{1,0:T(8,128)(2,1)S(1)}, bf16[128,1536]{1,0:T(8,128)(2,1)S(1)}, u32[]{:S(2)}, u32[]{:S(2)}) %collective-permute-start.5) | collective-permute-done | bytes 393248 | tf_op jit(solution)/shard_map/ppermute | solution.py:219
  31.9 1.3 %collective-permute-start.7 = (bf16[64,1536]{1,0:T(8,128)(2,1)S(1)}, bf16[64,1536]{1,0:T(8,128)(2,1)S(1)}, u32[]{:S(2)}, u32[]{:S(2)}) collective-permute-start(bf16[64,1536]{1,0:T(8,128)(2,1)S(1)} %get-tuple-element.49), channel_id=1, source_target_pairs={{0,4},{1,3},{2,6},{3,1},{4,0},{5,7},{6,2},{7,5},{8,12},{9,11},{10,... | collective-permute-start | bytes 589832 | tf_op jit(solution)/shard_map/ppermute | solution.py:219
  33.5 0.8 %collective-permute-start.6 = (f32[8,6784]{1,0:T(8,128)S(1)}, f32[8,6784]{1,0:T(8,128)S(1)}, u32[]{:S(2)}, u32[]{:S(2)}) collective-permute-start(f32[8,6784]{1,0:T(8,128)S(1)} %constant_dynamic-update-slice_fusion.5), channel_id=1, source_target_pairs={{0,4},{1,3},{2,6},{3,1},{4,0},{5,7},{6,2},{7,5},{8,12},{9,11},{10,... | collective-permute-start | bytes 651272 | tf_op jit(solution)/shard_map/ppermute | solution.py:219
  34.3 3.3 %collective-permute-done.7 = bf16[64,1536]{1,0:T(8,128)(2,1)S(1)} collective-permute-done((bf16[64,1536]{1,0:T(8,128)(2,1)S(1)}, bf16[64,1536]{1,0:T(8,128)(2,1)S(1)}, u32[]{:S(2)}, u32[]{:S(2)}) %collective-permute-start.7) | collective-permute-done | bytes 196640 | tf_op jit(solution)/shard_map/ppermute | solution.py:219
  37.8 2.2 %collective-permute-done.6 = f32[8,6784]{1,0:T(8,128)S(1)} collective-permute-done((f32[8,6784]{1,0:T(8,128)S(1)}, f32[8,6784]{1,0:T(8,128)S(1)}, u32[]{:S(2)}, u32[]{:S(2)}) %collective-permute-start.6) | collective-permute-done | bytes 217120 | tf_op jit(solution)/shard_map/ppermute | solution.py:219
  40.1 0.8 %collective-permute-start.8 = (f32[8,9344]{1,0:T(8,128)S(1)}, f32[8,9344]{1,0:T(8,128)S(1)}, u32[]{:S(2)}, u32[]{:S(2)}) collective-permute-start(f32[8,9344]{1,0:T(8,128)S(1)} %get-tuple-element.59), channel_id=1, source_target_pairs={{0,2},{1,5},{2,0},{3,7},{4,6},{5,1},{6,4},{7,3},{8,10},{9,13},{10,... | collective-permute-start | bytes 897032 | tf_op jit(solution)/shard_map/ppermute | solution.py:219
  41.5 1.7 %collective-permute-start.11 = (bf16[16,2560]{1,0:T(8,128)(2,1)S(1)}, bf16[16,2560]{1,0:T(8,128)(2,1)S(1)}, u32[]{:S(2)}, u32[]{:S(2)}) collective-permute-start(bf16[16,2560]{1,0:T(8,128)(2,1)S(1)} %get-tuple-element.55), channel_id=1, source_target_pairs={{0,16},{1,9},{2,18},{3,11},{4,20},{5,13},{6,22},{7,15},{8,24},{9,1... | collective-permute-start | bytes 245768 | tf_op jit(solution)/shard_map/ppermute | solution.py:219
  43.2 2.4 %collective-permute-start.12 = (bf16[16,1536]{1,0:T(8,128)(2,1)S(1)}, bf16[16,1536]{1,0:T(8,128)(2,1)S(1)}, u32[]{:S(2)}, u32[]{:S(2)}) collective-permute-start(bf16[16,1536]{1,0:T(8,128)(2,1)S(1)} %get-tuple-element.57), channel_id=1, source_target_pairs={{0,16},{1,9},{2,18},{3,11},{4,20},{5,13},{6,22},{7,15},{8,24},{9,1... | collective-permute-start | bytes 147464 | tf_op jit(solution)/shard_map/ppermute | solution.py:219
  45.6 1.4 %collective-permute-done.8 = f32[8,9344]{1,0:T(8,128)S(1)} collective-permute-done((f32[8,9344]{1,0:T(8,128)S(1)}, f32[8,9344]{1,0:T(8,128)S(1)}, u32[]{:S(2)}, u32[]{:S(2)}) %collective-permute-start.8) | collective-permute-done | bytes 299040 | tf_op jit(solution)/shard_map/ppermute | solution.py:219
  47.5 0.8 %collective-permute-done.12.refs_3_ = bf16[16,1536]{1,0:T(8,128)(2,1)S(1)} collective-permute-done((bf16[16,1536]{1,0:T(8,128)(2,1)S(1)}, bf16[16,1536]{1,0:T(8,128)(2,1)S(1)}, u32[]{:S(2)}, u32[]{:S(2)}) %collective-permute-start.12) | collective-permute-done | bytes 49184 | tf_op jit(solution)/shard_map/ppermute | solution.py:219
  48.3 1.2 %finish.1 = (f32[16,4096]{1,0:T(8,128)}, f32[8,4096]{1,0:T(8,128)}) custom-call(f32[8,4224]{1,0:T(8,128)S(1)} %slice_add_fusion.sums_ref, f32[16,16]{1,0:T(8,128)S(1)} %bitcast.13, f32[16,4096]{1,0:T(8,128)S(1)} %bitcast.12, f32[16,2560]{1,0:T(8,128)S(1)} %get-tuple-element.54.refs_0_, f32[16,1536]{1,0:T(8,128)S(1)} %get-tuple-element.56.refs_1_, ...), custom_call_target="tpu_custom_call" | custom-call | tf_op jit(solution)/shard_map/finish/pallas_call | solution.py:185
  (43 shorter events, 1.7 us)
Async XLA Ops:
  1.7 2.1 %collective-permute-start = (bf16[2048,128]{1,0:T(8,128)(2,1)S(1)}, bf16[2048,128]{1,0:T(8,128)(2,1)S(1)}, u32[]{:S(2)}, u32[]{:S(2)}) collective-permute-start(bf16[2048,128]{1,0:T(8,128)(2,1)S(1)} %slice.46.refs_0_), channel_id=1, source_target_pairs={{0,1},{1,0},{2,3},{3,2},{4,5},{5,4},{6,7},{7,6},{8,9},{9,8},{10,11... | collective-permute-start | bytes 1572872 | tf_op jit(solution)/shard_map/ppermute | solution.py:223
  11.1 11.5 %collective-permute-start.2 = (bf16[128,2560]{1,0:T(8,128)(2,1)S(1)}, bf16[128,2560]{1,0:T(8,128)(2,1)S(1)}, u32[]{:S(2)}, u32[]{:S(2)}) collective-permute-start(bf16[128,2560]{1,0:T(8,128)(2,1)S(1)} %get-tuple-element.32), channel_id=1, source_target_pairs={{0,2},{1,5},{2,0},{3,7},{4,6},{5,1},{6,4},{7,3},{8,10},{9,13},{10,... | collective-permute-start | bytes 1966088 | tf_op jit(solution)/shard_map/ppermute | solution.py:219
  19.0 6.6 %collective-permute-start.1 = (f32[8,4864]{1,0:T(8,128)S(1)}, f32[8,4864]{1,0:T(8,128)S(1)}, u32[]{:S(2)}, u32[]{:S(2)}) collective-permute-start(f32[8,4864]{1,0:T(8,128)S(1)} %get-tuple-element.69), channel_id=1, source_target_pairs={{0,8},{1,17},{2,10},{3,19},{4,12},{5,21},{6,14},{7,23},{8,0},{9,25... | collective-permute-start | bytes 466952 | tf_op jit(solution)/shard_map/ppermute | solution.py:219
  20.6 11.2 %collective-permute-start.5 = (bf16[128,1536]{1,0:T(8,128)(2,1)S(1)}, bf16[128,1536]{1,0:T(8,128)(2,1)S(1)}, u32[]{:S(2)}, u32[]{:S(2)}) collective-permute-start(bf16[128,1536]{1,0:T(8,128)(2,1)S(1)} %get-tuple-element.35), channel_id=1, source_target_pairs={{0,2},{1,5},{2,0},{3,7},{4,6},{5,1},{6,4},{7,3},{8,10},{9,13},{10,... | collective-permute-start | bytes 1179656 | tf_op jit(solution)/shard_map/ppermute | solution.py:219
  22.7 10.5 %collective-permute-start.4 = (bf16[64,2560]{1,0:T(8,128)(2,1)S(1)}, bf16[64,2560]{1,0:T(8,128)(2,1)S(1)}, u32[]{:S(2)}, u32[]{:S(2)}) collective-permute-start(bf16[64,2560]{1,0:T(8,128)(2,1)S(1)} %get-tuple-element.47), channel_id=1, source_target_pairs={{0,4},{1,3},{2,6},{3,1},{4,0},{5,7},{6,2},{7,5},{8,12},{9,11},{10,... | collective-permute-start | bytes 983048 | tf_op jit(solution)/shard_map/ppermute | solution.py:219
  25.7 7.7 %collective-permute-start.3 = (f32[8,5504]{1,0:T(8,128)S(1)}, f32[8,5504]{1,0:T(8,128)S(1)}, u32[]{:S(2)}, u32[]{:S(2)}) collective-permute-start(f32[8,5504]{1,0:T(8,128)S(1)} %pad_maximum_fusion), channel_id=1, source_target_pairs={{0,16},{1,9},{2,18},{3,11},{4,20},{5,13},{6,22},{7,15},{8,24},{9,1... | collective-permute-start | bytes 528392 | tf_op jit(solution)/shard_map/ppermute | solution.py:219
  31.9 5.7 %collective-permute-start.7 = (bf16[64,1536]{1,0:T(8,128)(2,1)S(1)}, bf16[64,1536]{1,0:T(8,128)(2,1)S(1)}, u32[]{:S(2)}, u32[]{:S(2)}) collective-permute-start(bf16[64,1536]{1,0:T(8,128)(2,1)S(1)} %get-tuple-element.49), channel_id=1, source_target_pairs={{0,4},{1,3},{2,6},{3,1},{4,0},{5,7},{6,2},{7,5},{8,12},{9,11},{10,... | collective-permute-start | bytes 589832 | tf_op jit(solution)/shard_map/ppermute | solution.py:219
  33.3 8.1 %collective-permute-start.10 = (bf16[32,2560]{1,0:T(8,128)(2,1)S(1)}, bf16[32,2560]{1,0:T(8,128)(2,1)S(1)}, u32[]{:S(2)}, u32[]{:S(2)}) collective-permute-start(bf16[32,2560]{1,0:T(8,128)(2,1)S(1)} %get-tuple-element.51), channel_id=1, source_target_pairs={{0,8},{1,17},{2,10},{3,19},{4,12},{5,21},{6,14},{7,23},{8,0},{9,25... | collective-permute-start | bytes 491528 | tf_op jit(solution)/shard_map/ppermute | solution.py:219
  33.5 6.5 %collective-permute-start.6 = (f32[8,6784]{1,0:T(8,128)S(1)}, f32[8,6784]{1,0:T(8,128)S(1)}, u32[]{:S(2)}, u32[]{:S(2)}) collective-permute-start(f32[8,6784]{1,0:T(8,128)S(1)} %constant_dynamic-update-slice_fusion.5), channel_id=1, source_target_pairs={{0,4},{1,3},{2,6},{3,1},{4,0},{5,7},{6,2},{7,5},{8,12},{9,11},{10,... | collective-permute-start | bytes 651272 | tf_op jit(solution)/shard_map/ppermute | solution.py:219
  37.7 5.4 %collective-permute-start.9 = (bf16[32,1536]{1,0:T(8,128)(2,1)S(1)}, bf16[32,1536]{1,0:T(8,128)(2,1)S(1)}, u32[]{:S(2)}, u32[]{:S(2)}) collective-permute-start(bf16[32,1536]{1,0:T(8,128)(2,1)S(1)} %get-tuple-element.53), channel_id=1, source_target_pairs={{0,8},{1,17},{2,10},{3,19},{4,12},{5,21},{6,14},{7,23},{8,0},{9,25... | collective-permute-start | bytes 294920 | tf_op jit(solution)/shard_map/ppermute | solution.py:219
  40.1 6.8 %collective-permute-start.8 = (f32[8,9344]{1,0:T(8,128)S(1)}, f32[8,9344]{1,0:T(8,128)S(1)}, u32[]{:S(2)}, u32[]{:S(2)}) collective-permute-start(f32[8,9344]{1,0:T(8,128)S(1)} %get-tuple-element.59), channel_id=1, source_target_pairs={{0,2},{1,5},{2,0},{3,7},{4,6},{5,1},{6,4},{7,3},{8,10},{9,13},{10,... | collective-permute-start | bytes 897032 | tf_op jit(solution)/shard_map/ppermute | solution.py:219
  41.5 6.8 %collective-permute-start.11 = (bf16[16,2560]{1,0:T(8,128)(2,1)S(1)}, bf16[16,2560]{1,0:T(8,128)(2,1)S(1)}, u32[]{:S(2)}, u32[]{:S(2)}) collective-permute-start(bf16[16,2560]{1,0:T(8,128)(2,1)S(1)} %get-tuple-element.55), channel_id=1, source_target_pairs={{0,16},{1,9},{2,18},{3,11},{4,20},{5,13},{6,22},{7,15},{8,24},{9,1... | collective-permute-start | bytes 245768 | tf_op jit(solution)/shard_map/ppermute | solution.py:219
  43.2 5.1 %collective-permute-start.12 = (bf16[16,1536]{1,0:T(8,128)(2,1)S(1)}, bf16[16,1536]{1,0:T(8,128)(2,1)S(1)}, u32[]{:S(2)}, u32[]{:S(2)}) collective-permute-start(bf16[16,1536]{1,0:T(8,128)(2,1)S(1)} %get-tuple-element.57), channel_id=1, source_target_pairs={{0,16},{1,9},{2,18},{3,11},{4,20},{5,13},{6,22},{7,15},{8,24},{9,1... | collective-permute-start | bytes 147464 | tf_op jit(solution)/shard_map/ppermute | solution.py:219
